TPU v7x, 32 devices: a whole 2x2x4 slice. The times are simulated.
32 devices in a mesh: gx: 16 (over z, y, core), gy: 2 (over x).
Axes of the slice: x: 2, y: 2, z: 4, core: 2. Of those that a mesh axis runs over, the one named last changes fastest.
Arguments:
- row_cells: int32 [2, 16, 4096], P('gy', 'gx'), may hold values from 0 to 255
- col_cells: int32 [2, 16, 4096], P('gy', 'gx'), may hold values from 0 to 255
- fracs: float32 [2, 2, 16, 4096], P(None, 'gy', 'gx'), may hold values from 0 to 1
- counts: int32 [2, 16], P('gy', 'gx'), may hold values from 512 to 4096, as said below
- targets: float32 [2, 16, 4096], P('gy', 'gx'), may hold values from -18 to 18
- amplitude: float32 [512, 4096], P('gy', 'gx'), may hold values from 0.5 to 2
- lengthscale: float32 [2], replicated, may hold values from 51.2 to 64
- ridge: float32 [1], replicated, may hold values from 0.5 to 2
Outputs:
- solution: float32 [2, 16, 4096], P('gy', 'gx')
- residual: float32 [2, 16, 4096], P('gy', 'gx')
- relative: float32 [1], replicated
Inputs may be any that keep to these rules, and one draw needn't show every extreme that they name: Slots 0 to counts - 1 of a tile are live; some tile holds 4096 live points.
All inputs are finite; a program needn't handle non-finite values.
Results may differ from a plain program's by a relative error of at most 0.0003.
Values sent between devices are 32-bit elements; how exact they have to be, the bound alone decides.
A program may use at most 64 MiB of HBM per device.

v0:
```python
import functools

import jax
import jax.numpy as jnp
from jax import lax
from jax.experimental import pallas as pl
from jax.experimental.pallas import tpu as pltpu
from jax.sharding import PartitionSpec as P

HB = 128
CHUNK = 512
MESH = pl.DeviceIdType.MESH
F32 = jnp.float32
BF16 = jnp.bfloat16


def up_to(value, step):
    return (value + step - 1) // step * step


def cubic_weights(fraction):
    square = fraction * fraction
    cube = square * fraction
    return (
        -0.5 * cube + square - 0.5 * fraction,
        1.5 * cube - 2.5 * square + 1.0,
        -1.5 * cube + 2.0 * square + 0.5 * fraction,
        0.5 * cube - 0.5 * square,
    )


def halves(value):
    high = value.astype(BF16)
    return high, (value - high.astype(F32)).astype(BF16)


def product(left, right, dims):
    def part(a, b):
        return lax.dot_general(a, b, (dims, ((), ())), preferred_element_type=F32)

    return part(left[0], right[0]) + part(left[1], right[0]) + part(left[0], right[1])


NN = ((1,), (0,))
NT = ((1,), (1,))


def band(source, target, scale, valid):
    distance = (source - target).astype(F32)
    kept = jnp.where(jnp.abs(distance) <= HB, jnp.exp(-distance * distance / (2.0 * scale * scale)), 0.0)
    return jnp.where(valid, kept, 0.0)


def kernel(
    n_gx, n_gy, rows, cols, slots,
    counts, lengthscale, ridge_ref, row_cells, col_cells, fracs, targets, amp,
    sol_ref, res_ref, rel_ref,
    rt, ct_hi, ct_lo, bc_hi, bc_lo, br_hi, br_lo, amp_ext, acc, vec,
    amp_lo, amp_hi, amp_wide, amp_up, amp_down,
    col_out, col_in, row_out, row_in, sum_out, sum_in,
    amp_send, amp_recv, ex_send, ex_recv, sum_send, sum_recv,
):
    n = n_gx * n_gy
    gx, gy = lax.axis_index("gx"), lax.axis_index("gy")
    me = gx * n_gy + gy
    right = {"gx": lax.rem(gx + 1, n_gx)}
    left = {"gx": lax.rem(gx + n_gx - 1, n_gx)}
    down = {"gy": lax.rem(gy + 1, n_gy)}
    up = {"gy": lax.rem(gy + n_gy - 1, n_gy)}
    er, ec = rt.shape[0], ct_hi.shape[0]
    ct_rows = up_to(cols + 3, 16)
    row_part = row_out.shape[2]

    barrier = pltpu.get_barrier_semaphore()

    def greet(k, carry):
        peer = lax.rem(me + k, n)
        pl.semaphore_signal(
            barrier, inc=1, device_id={"gx": peer // n_gy, "gy": lax.rem(peer, n_gy)}, device_id_type=MESH
        )
        return carry

    lax.fori_loop(1, n, greet, 0)
    pl.semaphore_wait(barrier, n - 1)

    def copy(source, dest, send, recv, to):
        return pltpu.make_async_remote_copy(
            src_ref=source, dst_ref=dest, send_sem=send, recv_sem=recv, device_id=to, device_id_type=MESH
        )

    amp_copies = [
        copy(amp.at[:, pl.ds(0, HB)], amp_hi, amp_send.at[0], amp_recv.at[0], left),
        copy(amp.at[:, pl.ds(cols - HB, HB)], amp_lo, amp_send.at[1], amp_recv.at[1], right),
    ]
    for item in amp_copies:
        item.start()

    source = lax.broadcasted_iota(jnp.int32, bc_hi.shape, 0)
    column = lax.broadcasted_iota(jnp.int32, bc_hi.shape, 1)
    to_left, to_right = column >= ec, column >= ec + 2 * HB
    target = jnp.where(to_right, column - ec - 2 * HB, jnp.where(to_left, column - ec + cols - HB, column))
    valid = (source < cols + 3) & (target < cols + 3)
    target = target + jnp.where(to_right, cols, jnp.where(to_left, -cols, 0))
    bc_hi[...], bc_lo[...] = halves(band(source, target, lengthscale[1], valid))

    source = lax.broadcasted_iota(jnp.int32, br_hi.shape, 1)
    row = lax.broadcasted_iota(jnp.int32, br_hi.shape, 0)
    to_up, to_down = row >= er, row >= er + row_part
    target = jnp.where(to_down, row - er - row_part, jnp.where(to_up, row - er + rows - HB, row))
    valid = (source < rows + 3) & (target < rows + 3)
    target = target + jnp.where(to_down, rows, jnp.where(to_up, -rows, 0))
    br_hi[...], br_lo[...] = halves(band(source, target, lengthscale[0], valid))

    for item in amp_copies:
        item.wait()
    joined = jnp.concatenate([amp_lo[...], amp[...], amp_hi[...]], axis=1)
    amp_wide[...] = pltpu.roll(joined, joined.shape[1] - (HB - 1), 1)[:, :ec]
    amp_rows = [
        copy(amp_wide.at[pl.ds(0, 8)], amp_down, amp_send.at[2], amp_recv.at[2], up),
        copy(amp_wide.at[pl.ds(rows - 8, 8)], amp_up, amp_send.at[3], amp_recv.at[3], down),
    ]
    for item in amp_rows:
        item.start()

    ct_hi[pl.ds(ct_rows, ec - ct_rows), :] = jnp.zeros((ec - ct_rows, slots), BF16)
    ct_lo[pl.ds(ct_rows, ec - ct_rows), :] = jnp.zeros((ec - ct_rows, slots), BF16)

    def chunk(i):
        return pl.ds(pl.multiple_of(i * CHUNK, CHUNK), CHUNK)

    def place(cells, fraction, length):
        index = lax.broadcasted_iota(jnp.int32, (length, CHUNK), 0) - cells
        weights = cubic_weights(fraction)
        out = jnp.zeros((length, CHUNK), F32)
        for offset in range(4):
            out = jnp.where(index == offset, weights[offset], out)
        return out

    def build(i, carry):
        at = chunk(i)
        live = (lax.broadcasted_iota(jnp.int32, (1, CHUNK), 1) + i * CHUNK < counts[0, 0]).astype(F32)
        rt[:, at] = place(row_cells[:, at], fracs[pl.ds(0, 1), at], er) * live
        high, low = halves(place(col_cells[:, at], fracs[pl.ds(1, 1), at], ct_rows))
        ct_hi[pl.ds(0, ct_rows), at] = high
        ct_lo[pl.ds(0, ct_rows), at] = low
        vec[pl.ds(0, 1), at] = targets[:, at] * live
        return carry

    lax.fori_loop(0, slots // CHUNK, build, 0)

    for item in amp_rows:
        item.wait()
    joined = jnp.concatenate([amp_up[...], amp_wide[...], amp_down[...]], axis=0)
    amp_ext[...] = pltpu.roll(joined, joined.shape[0] - 7, 0)[:er]

    ridge = ridge_ref[0]

    def operator_apply(step):
        acc[...] = jnp.zeros_like(acc)

        def spread(i, carry):
            at = chunk(i)
            scaled = halves(rt[:, at] * vec[pl.ds(step, 1), at])
            acc[...] += product(scaled, (ct_hi[:, at], ct_lo[:, at]), NT)
            return carry

        lax.fori_loop(0, slots // CHUNK, spread, 0)
        field = halves(amp_ext[...] * acc[...])
        sides = product(field, (bc_hi[:, pl.ds(ec, 4 * HB)], bc_lo[:, pl.ds(ec, 4 * HB)]), NN)
        col_out[step, 0] = sides[:, : 2 * HB]
        col_out[step, 1] = sides[:, 2 * HB :]
        copies = [
            copy(col_out.at[step, 0], col_in.at[step, 0], ex_send.at[4 * step], ex_recv.at[4 * step], left),
            copy(col_out.at[step, 1], col_in.at[step, 1], ex_send.at[4 * step + 1], ex_recv.at[4 * step + 1], right),
        ]
        for item in copies:
            item.start()
        acc[...] = product(field, (bc_hi[:, pl.ds(0, ec)], bc_lo[:, pl.ds(0, ec)]), NN)
        for item in copies:
            item.wait()
        acc[:, pl.ds(cols - HB, 2 * HB)] += col_in[step, 0]
        acc[:, pl.ds(0, 2 * HB)] += col_in[step, 1]
        across = halves(acc[...])
        count = 2 * row_part
        sides = product((br_hi[pl.ds(er, count), :], br_lo[pl.ds(er, count), :]), across, NN)
        row_out[step, 0] = sides[:row_part]
        row_out[step, 1] = sides[row_part:]
        copies = [
            copy(row_out.at[step, 0], row_in.at[step, 0], ex_send.at[4 * step + 2], ex_recv.at[4 * step + 2], up),
            copy(row_out.at[step, 1], row_in.at[step, 1], ex_send.at[4 * step + 3], ex_recv.at[4 * step + 3], down),
        ]
        for item in copies:
            item.start()
        acc[...] = product((br_hi[pl.ds(0, er), :], br_lo[pl.ds(0, er), :]), across, NN)
        for item in copies:
            item.wait()
        acc[pl.ds(rows - HB, row_part), :] += row_in[step, 0]
        acc[pl.ds(0, row_part), :] += row_in[step, 1]
        grid = halves(amp_ext[...] * acc[...])

        def gather(i, carry):
            at = chunk(i)
            picked = product(grid, (ct_hi[:, at], ct_lo[:, at]), NN)
            found = jnp.sum(picked * rt[:, at], axis=0, keepdims=True)
            vec[pl.ds(step + 1, 1), at] = found + ridge * vec[pl.ds(step, 1), at]
            return carry

        lax.fori_loop(0, slots // CHUNK, gather, 0)

    def lanes(value):
        total = value[:, :128]
        for at in range(1, slots // 128):
            total = total + value[:, at * 128 : (at + 1) * 128]
        return total

    def send_sums(which, values):
        for q, value in enumerate(values):
            sum_out[which, pl.ds(q, 1), :] = lanes(value)
        sum_in[which, me] = sum_out[which]

        def one(k, carry):
            peer = lax.rem(me + k, n)
            copy(
                sum_out.at[which], sum_in.at[which, me], sum_send.at[which], sum_recv.at[which],
                {"gx": peer // n_gy, "gy": lax.rem(peer, n_gy)},
            ).start()
            return carry

        lax.fori_loop(1, n, one, 0)

    def take_sums(which, count):
        others = sum_in.at[which, pl.ds(0, n - 1)]
        pltpu.make_async_copy(others, others, sum_recv.at[which]).wait()
        pltpu.make_async_copy(others, others, sum_send.at[which]).wait()
        total = jnp.sum(sum_in[which], axis=0)
        return [jnp.sum(total[q : q + 1, :]) for q in range(count)]

    sum_out[...] = jnp.zeros_like(sum_out)
    operator_apply(0)
    right_side, image = vec[pl.ds(0, 1), :], vec[pl.ds(1, 1), :]
    send_sums(0, [right_side * right_side, right_side * image])
    operator_apply(1)
    norm_start, first = take_sums(0, 2)
    right_side, image = vec[pl.ds(0, 1), :], vec[pl.ds(1, 1), :]
    step_one = norm_start / first
    residual_one = right_side - step_one * image
    response = image - step_one * vec[pl.ds(2, 1), :]
    send_sums(1, [residual_one * residual_one, residual_one * response])
    norm_mid, second = take_sums(1, 2)
    ratio = norm_mid / norm_start
    direction = residual_one + ratio * right_side
    image_two = response + ratio * image
    step_two = norm_mid / (second - ratio * norm_mid / step_one)
    residual = residual_one - step_two * image_two
    sol_ref[...] = step_one * right_side + step_two * direction
    res_ref[...] = residual
    send_sums(2, [residual * residual])
    (norm_end,) = take_sums(2, 1)
    rel_ref[0] = norm_end / norm_start


def shards(n_gx, n_gy, row_cells, col_cells, fracs, counts, targets, amplitude, lengthscale, ridge):
    rows, cols = amplitude.shape
    slots = targets.shape[2]
    n = n_gx * n_gy
    er, ec = up_to(rows + 3, 16), up_to(cols + 3, 128)
    row_part = up_to(HB + 3, 8)
    vmem = pl.BlockSpec(memory_space=pltpu.VMEM)
    smem = pl.BlockSpec(memory_space=pltpu.SMEM)
    sol, res, rel = pl.pallas_call(
        functools.partial(kernel, n_gx, n_gy, rows, cols, slots),
        out_shape=(
            jax.ShapeDtypeStruct((1, slots), F32),
            jax.ShapeDtypeStruct((1, slots), F32),
            jax.ShapeDtypeStruct((1,), F32),
        ),
        in_specs=[smem] * 3 + [vmem] * 5,
        out_specs=(vmem, vmem, smem),
        scratch_shapes=[
            pltpu.VMEM((er, slots), F32),
            pltpu.VMEM((ec, slots), BF16),
            pltpu.VMEM((ec, slots), BF16),
            pltpu.VMEM((ec, ec + 4 * HB), BF16),
            pltpu.VMEM((ec, ec + 4 * HB), BF16),
            pltpu.VMEM((er + 2 * row_part, er), BF16),
            pltpu.VMEM((er + 2 * row_part, er), BF16),
            pltpu.VMEM((er, ec), F32),
            pltpu.VMEM((er, ec), F32),
            pltpu.VMEM((8, slots), F32),
            pltpu.VMEM((rows, HB), F32),
            pltpu.VMEM((rows, HB), F32),
            pltpu.VMEM((rows, ec), F32),
            pltpu.VMEM((8, ec), F32),
            pltpu.VMEM((8, ec), F32),
            pltpu.VMEM((2, 2, er, 2 * HB), F32),
            pltpu.VMEM((2, 2, er, 2 * HB), F32),
            pltpu.VMEM((2, 2, row_part, ec), F32),
            pltpu.VMEM((2, 2, row_part, ec), F32),
            pltpu.VMEM((3, 8, 128), F32),
            pltpu.VMEM((3, n, 8, 128), F32),
            pltpu.SemaphoreType.DMA((4,)),
            pltpu.SemaphoreType.DMA((4,)),
            pltpu.SemaphoreType.DMA((8,)),
            pltpu.SemaphoreType.DMA((8,)),
            pltpu.SemaphoreType.DMA((3,)),
            pltpu.SemaphoreType.DMA((3,)),
        ],
        compiler_params=pltpu.CompilerParams(
            collective_id=0, has_side_effects=True, vmem_limit_bytes=48 * 1024 * 1024
        ),
    )(
        counts, lengthscale, ridge,
        row_cells[0], col_cells[0], fracs[:, 0, 0], targets[0], amplitude,
    )
    return sol[None], res[None], rel


def solution(mesh):
    placed = (
        P("gy", "gx", None),
        P("gy", "gx", None),
        P(None, "gy", "gx", None),
        P("gy", "gx"),
        P("gy", "gx", None),
        P("gy", "gx"),
        P(),
        P(),
    )
    return jax.shard_map(
        functools.partial(shards, mesh.shape["gx"], mesh.shape["gy"]),
        mesh=mesh,
        in_specs=placed,
        out_specs=(P("gy", "gx", None), P("gy", "gx", None), P()),
        check_vma=False,
    )
```

profile of v0, /device:TPU:0, one launch (start us, length us, event | category | flops | bytes accessed | tf_op | source)
XLA Modules:
  0.0 91.3 jit_solution(17572889766546789339)
XLA Ops:
  1.9 0.0 copy-start.1
  1.9 0.0 copy-start.2
  1.9 0.0 copy-start.3
  2.0 0.8 copy.13
  2.8 0.0 copy-start.4
  2.8 0.0 copy-done.1
  2.8 0.0 copy-done.2
  2.8 0.0 copy-done.3
  2.8 0.6 copy-done.4
  3.4 0.0 copy-start
  3.4 0.9 %copy-done = f32[256,256]{1,0:T(8,128)S(1)} copy-done((f32[256,256]{1,0:T(8,128)S(1)}, f32[256,256]{1,0:T(8,128)}, u32[]{:S(2)}) %copy-start) | copy-done | bytes 262168
  4.4 84.0 %shard_map.103 = (f32[1,4096]{1,0:T(1,128)S(1)}, f32[1,4096]{1,0:T(1,128)S(1)}, f32[1]{0:T(128)}) custom-call(s32[1,1]{1,0:T(1,128)S(6)} %copy.17.counts, f32[2]{0:T(128)S(1)} %copy-done.4, f32[1]{0:T(128)S(6)} %copy.18.ridge_ref, s32[1,4096]{1,0:T(1,128)S(1)} %bitcast.11, s32[1,4096]{1,0:T(1,128)S(1)} %bitcast.12, f32[2,4096]{1,0:T(2,128)S(1)} %bitcast.8, ...), custom_call_target="tpu_custom_call" | custom-call | tf_op jit(solution)/shard_map/pallas_call | solution.py:270
  88.4 0.6 copy.19
  89.0 0.6 copy.20
Async XLA Ops:
  1.9 0.8 copy-start.1
  1.9 0.8 copy-start.2
  1.9 0.8 copy-start.3
  2.8 0.7 copy-start.4
  3.4 0.9 %copy-start = (f32[256,256]{1,0:T(8,128)S(1)}, f32[256,256]{1,0:T(8,128)}, u32[]{:S(2)}) copy-start(f32[256,256]{1,0:T(8,128)} %amp.1) | copy-start | bytes 786436
where the time goes:
time: 91.6 us; the launch traced here: 91.3 us
  Pallas kernels  84 us (92%)
  between operations  3.68 us (4%)
  local copies, waits for them, and re-layouts  3.6 us (4%)
    pallas_call x1, Pallas kernels, shards(): pl.pallas_call(functools.partial(kernel, n_gx, n_gy, rows, cols, slots),...  84 us
    unnamed x13, local copies, waits for them, and re-layouts  3.6 us

commit v1 on v0

--- a/solution.py
+++ b/solution.py
@@ -8,7 +8,8 @@
 from jax.sharding import PartitionSpec as P
 
 HB = 128
-CHUNK = 512
+CHUNK = 2048
+BUILD = 512
 MESH = pl.DeviceIdType.MESH
 F32 = jnp.float32
 BF16 = jnp.bfloat16
@@ -55,10 +56,10 @@
     n_gx, n_gy, rows, cols, slots,
     counts, lengthscale, ridge_ref, row_cells, col_cells, fracs, targets, amp,
     sol_ref, res_ref, rel_ref,
-    rt, ct_hi, ct_lo, bc_hi, bc_lo, br_hi, br_lo, amp_ext, acc, vec,
+    rt, ct_hi, ct_lo, bc_hi, bc_lo, br_hi, br_lo, amp_ext, acc, smooth, vec,
     amp_lo, amp_hi, amp_wide, amp_up, amp_down,
     col_out, col_in, row_out, row_in, sum_out, sum_in,
-    amp_send, amp_recv, ex_send, ex_recv, sum_send, sum_recv,
+    amp_send, amp_recv, col_send, col_recv, row_send, row_recv, sum_send, sum_recv,
 ):
     n = n_gx * n_gy
     gx, gy = lax.axis_index("gx"), lax.axis_index("gy")
@@ -69,7 +70,11 @@
     up = {"gy": lax.rem(gy + n_gy - 1, n_gy)}
     er, ec = rt.shape[0], ct_hi.shape[0]
     ct_rows = up_to(cols + 3, 16)
-    row_part = row_out.shape[2]
+    row_part = row_out.shape[2] - 8
+    side = (br_hi.shape[0] - er) // 2
+
+    half = row_part
+    parts = (pl.ds(0, half), pl.ds(half, er - half))
 
     barrier = pltpu.get_barrier_semaphore()
 
@@ -81,19 +86,11 @@
         return carry
 
     lax.fori_loop(1, n, greet, 0)
-    pl.semaphore_wait(barrier, n - 1)
 
     def copy(source, dest, send, recv, to):
         return pltpu.make_async_remote_copy(
             src_ref=source, dst_ref=dest, send_sem=send, recv_sem=recv, device_id=to, device_id_type=MESH
         )
-
-    amp_copies = [
-        copy(amp.at[:, pl.ds(0, HB)], amp_hi, amp_send.at[0], amp_recv.at[0], left),
-        copy(amp.at[:, pl.ds(cols - HB, HB)], amp_lo, amp_send.at[1], amp_recv.at[1], right),
-    ]
-    for item in amp_copies:
-        item.start()
 
     source = lax.broadcasted_iota(jnp.int32, bc_hi.shape, 0)
     column = lax.broadcasted_iota(jnp.int32, bc_hi.shape, 1)
@@ -105,11 +102,43 @@
 
     source = lax.broadcasted_iota(jnp.int32, br_hi.shape, 1)
     row = lax.broadcasted_iota(jnp.int32, br_hi.shape, 0)
-    to_up, to_down = row >= er, row >= er + row_part
-    target = jnp.where(to_down, row - er - row_part, jnp.where(to_up, row - er + rows - HB, row))
+    to_up, to_down = row >= er, row >= er + side
+    target = jnp.where(to_down, row - er - side, jnp.where(to_up, row - er + rows - HB, row))
     valid = (source < rows + 3) & (target < rows + 3)
     target = target + jnp.where(to_down, rows, jnp.where(to_up, -rows, 0))
     br_hi[...], br_lo[...] = halves(band(source, target, lengthscale[0], valid))
+
+    pl.semaphore_wait(barrier, n - 1)
+    amp_copies = [
+        copy(amp.at[:, pl.ds(0, HB)], amp_hi, amp_send.at[0], amp_recv.at[0], left),
+        copy(amp.at[:, pl.ds(cols - HB, HB)], amp_lo, amp_send.at[1], amp_recv.at[1], right),
+    ]
+    for item in amp_copies:
+        item.start()
+
+    ct_hi[pl.ds(ct_rows, ec - ct_rows), :] = jnp.zeros((ec - ct_rows, slots), BF16)
+    ct_lo[pl.ds(ct_rows, ec - ct_rows), :] = jnp.zeros((ec - ct_rows, slots), BF16)
+
+    def place(cells, fraction, length):
+        index = lax.broadcasted_iota(jnp.int32, (length, BUILD), 0) - cells
+        weights = cubic_weights(fraction)
+        out = jnp.zeros((length, BUILD), F32)
+        for offset in range(4):
+            out = jnp.where(index == offset, weights[offset], out)
+        return out
+
+    def build(i, carry):
+        at = pl.ds(pl.multiple_of(i * BUILD, BUILD), BUILD)
+        live = (lax.broadcasted_iota(jnp.int32, (1, BUILD), 1) + i * BUILD < counts[0, 0]).astype(F32)
+        rt[:, at] = place(row_cells[:, at], fracs[pl.ds(0, 1), at], er) * live
+        high, low = halves(place(col_cells[:, at], fracs[pl.ds(1, 1), at], ct_rows))
+        ct_hi[pl.ds(0, ct_rows), at] = high
+        ct_lo[pl.ds(0, ct_rows), at] = low
+        vec[pl.ds(0, 1), at] = targets[:, at] * live
+        return carry
+
+    builds = slots // BUILD
+    lax.fori_loop(0, builds // 2, build, 0)
 
     for item in amp_copies:
         item.wait()
@@ -122,31 +151,7 @@
     for item in amp_rows:
         item.start()
 
-    ct_hi[pl.ds(ct_rows, ec - ct_rows), :] = jnp.zeros((ec - ct_rows, slots), BF16)
-    ct_lo[pl.ds(ct_rows, ec - ct_rows), :] = jnp.zeros((ec - ct_rows, slots), BF16)
-
-    def chunk(i):
-        return pl.ds(pl.multiple_of(i * CHUNK, CHUNK), CHUNK)
-
-    def place(cells, fraction, length):
-        index = lax.broadcasted_iota(jnp.int32, (length, CHUNK), 0) - cells
-        weights = cubic_weights(fraction)
-        out = jnp.zeros((length, CHUNK), F32)
-        for offset in range(4):
-            out = jnp.where(index == offset, weights[offset], out)
-        return out
-
-    def build(i, carry):
-        at = chunk(i)
-        live = (lax.broadcasted_iota(jnp.int32, (1, CHUNK), 1) + i * CHUNK < counts[0, 0]).astype(F32)
-        rt[:, at] = place(row_cells[:, at], fracs[pl.ds(0, 1), at], er) * live
-        high, low = halves(place(col_cells[:, at], fracs[pl.ds(1, 1), at], ct_rows))
-        ct_hi[pl.ds(0, ct_rows), at] = high
-        ct_lo[pl.ds(0, ct_rows), at] = low
-        vec[pl.ds(0, 1), at] = targets[:, at] * live
-        return carry
-
-    lax.fori_loop(0, slots // CHUNK, build, 0)
+    lax.fori_loop(builds // 2, builds, build, 0)
 
     for item in amp_rows:
         item.wait()
@@ -154,58 +159,91 @@
     amp_ext[...] = pltpu.roll(joined, joined.shape[0] - 7, 0)[:er]
 
     ridge = ridge_ref[0]
+    chunks = [pl.ds(at, CHUNK) for at in range(0, slots, CHUNK)]
+
+    def pack(edge):
+        total = edge[:8]
+        for i in range(1, edge.shape[0] // 8):
+            total = total + pltpu.roll(edge[8 * i : 8 * i + 8], 3 * i, 1)
+        return total
+
+    def unpack(packed, length):
+        first = lax.broadcasted_iota(jnp.int32, packed.shape, 1) < 3
+        return jnp.concatenate(
+            [jnp.where(first, pltpu.roll(packed, 128 - 3 * i, 1) if i else packed, 0.0) for i in range(length // 8)],
+            axis=0,
+        )
 
     def operator_apply(step):
-        acc[...] = jnp.zeros_like(acc)
-
-        def spread(i, carry):
-            at = chunk(i)
-            scaled = halves(rt[:, at] * vec[pl.ds(step, 1), at])
-            acc[...] += product(scaled, (ct_hi[:, at], ct_lo[:, at]), NT)
-            return carry
-
-        lax.fori_loop(0, slots // CHUNK, spread, 0)
-        field = halves(amp_ext[...] * acc[...])
-        sides = product(field, (bc_hi[:, pl.ds(ec, 4 * HB)], bc_lo[:, pl.ds(ec, 4 * HB)]), NN)
-        col_out[step, 0] = sides[:, : 2 * HB]
-        col_out[step, 1] = sides[:, 2 * HB :]
-        copies = [
-            copy(col_out.at[step, 0], col_in.at[step, 0], ex_send.at[4 * step], ex_recv.at[4 * step], left),
-            copy(col_out.at[step, 1], col_in.at[step, 1], ex_send.at[4 * step + 1], ex_recv.at[4 * step + 1], right),
-        ]
-        for item in copies:
+        col_copies = []
+
+        def spread(h):
+            total = None
+            for at in chunks:
+                scaled = halves(rt[parts[h], at] * vec[pl.ds(step, 1), at])
+                term = product(scaled, (ct_hi[:, at], ct_lo[:, at]), NT)
+                total = term if total is None else total + term
+            field = halves(amp_ext[parts[h], :] * total)
+            sides = product(field, (bc_hi[:, pl.ds(ec, 4 * HB)], bc_lo[:, pl.ds(ec, 4 * HB)]), NN)
+            length = sides.shape[0]
+            for d, to in enumerate((left, right)):
+                out = col_out.at[step, h, d]
+                out[pl.ds(0, length), :] = sides[:, 2 * HB * d : 2 * HB * d + HB]
+                out[pl.ds(length, 8), :] = pack(sides[:, 2 * HB * d + HB : 2 * HB * (d + 1)])
+                sem = 4 * step + 2 * h + d
+                item = copy(out, col_in.at[step, h, d], col_send.at[sem], col_recv.at[sem], to)
+                item.start()
+                col_copies.append(item)
+            acc[parts[h], :] = product(field, (bc_hi[:, pl.ds(0, ec)], bc_lo[:, pl.ds(0, ec)]), NN)
+
+        def collect(h):
+            length = half if h == 0 else er - half
+            for d in range(2):
+                col_copies[2 * h + d].wait()
+                start = cols - HB if d == 0 else 0
+                got = col_in.at[step, h, d]
+                acc[parts[h], pl.ds(start, HB)] += got[pl.ds(0, length), :]
+                acc[parts[h], pl.ds(start + HB, HB)] += unpack(got[pl.ds(length, 8), :], length)
+
+        def send_rows(d, to, low, count):
+            taps = (br_hi[pl.ds(er + side * d, side), pl.ds(low, count)], br_lo[pl.ds(er + side * d, side), pl.ds(low, count)])
+            piece = product(taps, halves(acc[pl.ds(low, count), :]), NN)
+            out = row_out.at[step, d]
+            out[pl.ds(0, row_part), :] = piece[:row_part, :cols]
+            out[pl.ds(row_part, 8), :] = jnp.zeros((8, cols), F32)
+            out[pl.ds(row_part, 8), pl.ds(0, 128)] = pack(piece[:row_part, cols:])
+            item = copy(out, row_in.at[step, d], row_send.at[2 * step + d], row_recv.at[2 * step + d], to)
             item.start()
-        acc[...] = product(field, (bc_hi[:, pl.ds(0, ec)], bc_lo[:, pl.ds(0, ec)]), NN)
-        for item in copies:
+            return item
+
+        def take_rows(d, item):
             item.wait()
-        acc[:, pl.ds(cols - HB, 2 * HB)] += col_in[step, 0]
-        acc[:, pl.ds(0, 2 * HB)] += col_in[step, 1]
-        across = halves(acc[...])
-        count = 2 * row_part
-        sides = product((br_hi[pl.ds(er, count), :], br_lo[pl.ds(er, count), :]), across, NN)
-        row_out[step, 0] = sides[:row_part]
-        row_out[step, 1] = sides[row_part:]
-        copies = [
-            copy(row_out.at[step, 0], row_in.at[step, 0], ex_send.at[4 * step + 2], ex_recv.at[4 * step + 2], up),
-            copy(row_out.at[step, 1], row_in.at[step, 1], ex_send.at[4 * step + 3], ex_recv.at[4 * step + 3], down),
-        ]
-        for item in copies:
-            item.start()
-        acc[...] = product((br_hi[pl.ds(0, er), :], br_lo[pl.ds(0, er), :]), across, NN)
-        for item in copies:
-            item.wait()
-        acc[pl.ds(rows - HB, row_part), :] += row_in[step, 0]
-        acc[pl.ds(0, row_part), :] += row_in[step, 1]
-        grid = halves(amp_ext[...] * acc[...])
-
-        def gather(i, carry):
-            at = chunk(i)
-            picked = product(grid, (ct_hi[:, at], ct_lo[:, at]), NN)
-            found = jnp.sum(picked * rt[:, at], axis=0, keepdims=True)
-            vec[pl.ds(step + 1, 1), at] = found + ridge * vec[pl.ds(step, 1), at]
-            return carry
-
-        lax.fori_loop(0, slots // CHUNK, gather, 0)
+            at = pl.ds(rows - HB, row_part) if d == 0 else pl.ds(0, row_part)
+            got = row_in.at[step, d]
+            smooth[at, pl.ds(0, cols)] += got[pl.ds(0, row_part), :]
+            smooth[at, pl.ds(cols, 128)] += unpack(got[pl.ds(row_part, 8), pl.ds(0, 128)], row_part)
+
+        def gather(h):
+            grid = halves(amp_ext[parts[h], :] * smooth[parts[h], :])
+            for at in chunks:
+                picked = product(grid, (ct_hi[:, at], ct_lo[:, at]), NN)
+                found = jnp.sum(picked * rt[parts[h], at], axis=0, keepdims=True)
+                if h == 1:
+                    vec[pl.ds(step + 1, 1), at] = found + ridge * vec[pl.ds(step, 1), at]
+                else:
+                    vec[pl.ds(step + 1, 1), at] += found
+
+        spread(0)
+        spread(1)
+        collect(0)
+        sent_up = send_rows(0, up, 0, half)
+        collect(1)
+        sent_down = send_rows(1, down, rows - HB, er - (rows - HB))
+        smooth[...] = product((br_hi[pl.ds(0, er), :], br_lo[pl.ds(0, er), :]), halves(acc[...]), NN)
+        take_rows(0, sent_up)
+        gather(1)
+        take_rows(1, sent_down)
+        gather(0)
 
     def lanes(value):
         total = value[:, :128]
@@ -282,8 +320,9 @@
             pltpu.VMEM((ec, slots), BF16),
             pltpu.VMEM((ec, ec + 4 * HB), BF16),
             pltpu.VMEM((ec, ec + 4 * HB), BF16),
-            pltpu.VMEM((er + 2 * row_part, er), BF16),
-            pltpu.VMEM((er + 2 * row_part, er), BF16),
+            pltpu.VMEM((er + 2 * up_to(HB + 3, 16), er), BF16),
+            pltpu.VMEM((er + 2 * up_to(HB + 3, 16), er), BF16),
+            pltpu.VMEM((er, ec), F32),
             pltpu.VMEM((er, ec), F32),
             pltpu.VMEM((er, ec), F32),
             pltpu.VMEM((8, slots), F32),
@@ -292,16 +331,18 @@
             pltpu.VMEM((rows, ec), F32),
             pltpu.VMEM((8, ec), F32),
             pltpu.VMEM((8, ec), F32),
-            pltpu.VMEM((2, 2, er, 2 * HB), F32),
-            pltpu.VMEM((2, 2, er, 2 * HB), F32),
-            pltpu.VMEM((2, 2, row_part, ec), F32),
-            pltpu.VMEM((2, 2, row_part, ec), F32),
+            pltpu.VMEM((2, 2, 2, max(row_part, er - row_part) + 8, HB), F32),
+            pltpu.VMEM((2, 2, 2, max(row_part, er - row_part) + 8, HB), F32),
+            pltpu.VMEM((2, 2, row_part + 8, cols), F32),
+            pltpu.VMEM((2, 2, row_part + 8, cols), F32),
             pltpu.VMEM((3, 8, 128), F32),
             pltpu.VMEM((3, n, 8, 128), F32),
             pltpu.SemaphoreType.DMA((4,)),
             pltpu.SemaphoreType.DMA((4,)),
             pltpu.SemaphoreType.DMA((8,)),
             pltpu.SemaphoreType.DMA((8,)),
+            pltpu.SemaphoreType.DMA((4,)),
+            pltpu.SemaphoreType.DMA((4,)),
             pltpu.SemaphoreType.DMA((3,)),
             pltpu.SemaphoreType.DMA((3,)),
         ],

time: 91.6 us -> 75.3 us (0.82)
  Pallas kernels: 84 us -> 67.7 us
    pallas_call x1, Pallas kernels: 84 us -> 67.7 us  [shards(): pl.pallas_call(functools.partial(kernel, n_gx, n_gy, rows, cols, slots),...]
where the time goes in v1:
time: 75.3 us; the launch traced here: 75 us
  Pallas kernels  67.7 us (90%)
  between operations  3.68 us (5%)
  local copies, waits for them, and re-layouts  3.6 us (5%)
    pallas_call x1, Pallas kernels, shards(): pl.pallas_call(functools.partial(kernel, n_gx, n_gy, rows, cols, slots),...  67.7 us
    unnamed x13, local copies, waits for them, and re-layouts  3.6 us

profile of v1, /device:TPU:0, one launch (start us, length us, event | category | flops | bytes accessed | tf_op | source)
XLA Modules:
  0.0 75.0 jit_solution(15205393274369549669)
XLA Ops:
  1.9 0.0 copy-start.1
  1.9 0.0 copy-start.2
  1.9 0.0 copy-start.3
  2.0 0.8 %copy.13 = f32[2,1,1,4096]{3,0,1,2:T(2,128)S(1)} copy(f32[2,1,1,4096]{3,2,1,0:T(1,128)} %param.10) | data formatting | bytes 65536
  2.8 0.0 copy-start.4
  2.8 0.0 copy-done.1
  2.8 0.0 copy-done.2
  2.8 0.0 copy-done.3
  2.8 0.6 copy-done.4
  3.4 0.0 copy-start
  3.4 0.9 %copy-done = f32[256,256]{1,0:T(8,128)S(1)} copy-done((f32[256,256]{1,0:T(8,128)S(1)}, f32[256,256]{1,0:T(8,128)}, u32[]{:S(2)}) %copy-start) | copy-done | bytes 262168
  4.4 67.7 %shard_map.103 = (f32[1,4096]{1,0:T(1,128)S(1)}, f32[1,4096]{1,0:T(1,128)S(1)}, f32[1]{0:T(128)}) custom-call(s32[1,1]{1,0:T(1,128)S(6)} %copy.17.counts, f32[2]{0:T(128)S(1)} %copy-done.4, f32[1]{0:T(128)S(6)} %copy.18.ridge_ref, s32[1,4096]{1,0:T(1,128)S(1)} %bitcast.11, s32[1,4096]{1,0:T(1,128)S(1)} %bitcast.12, f32[2,4096]{1,0:T(2,128)S(1)} %bitcast.8, ...), custom_call_target="tpu_custom_call" | custom-call | tf_op jit(solution)/shard_map/pallas_call | solution.py:308
  72.1 0.6 copy.19
  72.7 0.6 copy.20
Async XLA Ops:
  1.9 0.8 %copy-start.1 = (s32[1,1,4096]{2,1,0:T(1,128)S(1)}, s32[1,1,4096]{2,1,0:T(1,128)}, u32[]{:S(2)}) copy-start(s32[1,1,4096]{2,1,0:T(1,128)} %param.8) | copy-start | bytes 49156
  1.9 0.8 %copy-start.2 = (s32[1,1,4096]{2,1,0:T(1,128)S(1)}, s32[1,1,4096]{2,1,0:T(1,128)}, u32[]{:S(2)}) copy-start(s32[1,1,4096]{2,1,0:T(1,128)} %param.9) | copy-start | bytes 49156
  1.9 0.8 %copy-start.3 = (f32[1,1,4096]{2,1,0:T(1,128)S(1)}, f32[1,1,4096]{2,1,0:T(1,128)}, u32[]{:S(2)}) copy-start(f32[1,1,4096]{2,1,0:T(1,128)} %param.12) | copy-start | bytes 49156
  2.8 0.7 copy-start.4
  3.4 0.9 %copy-start = (f32[256,256]{1,0:T(8,128)S(1)}, f32[256,256]{1,0:T(8,128)}, u32[]{:S(2)}) copy-start(f32[256,256]{1,0:T(8,128)} %amp.1) | copy-start | bytes 786436

commit v2 on v1

--- a/solution.py
+++ b/solution.py
@@ -8,7 +8,7 @@
 from jax.sharding import PartitionSpec as P
 
 HB = 128
-CHUNK = 2048
+CHUNK = 4096
 BUILD = 512
 MESH = pl.DeviceIdType.MESH
 F32 = jnp.float32

time: 75.3 us -> 75.3 us (level)
  no operation moved by 1% of the time
where the time goes in v2:
time: 75.3 us; the launch traced here: 75 us
  Pallas kernels  67.7 us (90%)
  between operations  3.68 us (5%)
  local copies, waits for them, and re-layouts  3.6 us (5%)
    pallas_call x1, Pallas kernels, shards(): pl.pallas_call(functools.partial(kernel, n_gx, n_gy, rows, cols, slots),...  67.7 us
    unnamed x13, local copies, waits for them, and re-layouts  3.6 us

profile of v2, /device:TPU:0, one launch (start us, length us, event | category | flops | bytes accessed | tf_op | source)
XLA Modules:
  0.0 75.0 jit_solution(5485984972778362230)
XLA Ops:
  1.9 0.0 copy-start.1
  1.9 0.0 copy-start.2
  1.9 0.0 copy-start.3
  2.0 0.8 %copy.13 = f32[2,1,1,4096]{3,0,1,2:T(2,128)S(1)} copy(f32[2,1,1,4096]{3,2,1,0:T(1,128)} %param.10) | data formatting | bytes 65536
  2.8 0.0 copy-start.4
  2.8 0.0 copy-done.1
  2.8 0.0 copy-done.2
  2.8 0.0 copy-done.3
  2.8 0.6 copy-done.4
  3.4 0.0 copy-start
  3.4 0.9 %copy-done = f32[256,256]{1,0:T(8,128)S(1)} copy-done((f32[256,256]{1,0:T(8,128)S(1)}, f32[256,256]{1,0:T(8,128)}, u32[]{:S(2)}) %copy-start) | copy-done | bytes 262168
  4.4 67.7 %shard_map.103 = (f32[1,4096]{1,0:T(1,128)S(1)}, f32[1,4096]{1,0:T(1,128)S(1)}, f32[1]{0:T(128)}) custom-call(s32[1,1]{1,0:T(1,128)S(6)} %copy.17.counts, f32[2]{0:T(128)S(1)} %copy-done.4, f32[1]{0:T(128)S(6)} %copy.18.ridge_ref, s32[1,4096]{1,0:T(1,128)S(1)} %bitcast.11, s32[1,4096]{1,0:T(1,128)S(1)} %bitcast.12, f32[2,4096]{1,0:T(2,128)S(1)} %bitcast.8, ...), custom_call_target="tpu_custom_call" | custom-call | tf_op jit(solution)/shard_map/pallas_call | solution.py:308
  72.1 0.6 copy.19
  72.7 0.6 copy.20
Async XLA Ops:
  1.9 0.8 %copy-start.1 = (s32[1,1,4096]{2,1,0:T(1,128)S(1)}, s32[1,1,4096]{2,1,0:T(1,128)}, u32[]{:S(2)}) copy-start(s32[1,1,4096]{2,1,0:T(1,128)} %param.8) | copy-start | bytes 49156
  1.9 0.8 %copy-start.2 = (s32[1,1,4096]{2,1,0:T(1,128)S(1)}, s32[1,1,4096]{2,1,0:T(1,128)}, u32[]{:S(2)}) copy-start(s32[1,1,4096]{2,1,0:T(1,128)} %param.9) | copy-start | bytes 49156
  1.9 0.8 %copy-start.3 = (f32[1,1,4096]{2,1,0:T(1,128)S(1)}, f32[1,1,4096]{2,1,0:T(1,128)}, u32[]{:S(2)}) copy-start(f32[1,1,4096]{2,1,0:T(1,128)} %param.12) | copy-start | bytes 49156
  2.8 0.7 copy-start.4
  3.4 0.9 %copy-start = (f32[256,256]{1,0:T(8,128)S(1)}, f32[256,256]{1,0:T(8,128)}, u32[]{:S(2)}) copy-start(f32[256,256]{1,0:T(8,128)} %amp.1) | copy-start | bytes 786436
